TPU v7x, 512 devices: a whole 4x8x8 slice. The times are simulated.
512 devices in a mesh: rep: 32 (over y, x), tp: 16 (over z, core).
Axes of the slice: x: 4, y: 8, z: 8, core: 2. Of those that a mesh axis runs over, the one named last changes fastest.
Arguments:
- activations: bfloat16 [65536, 4096], P('rep', 'tp'), may hold values from -40 to 40
- out_grad: bfloat16 [65536, 1024], P(('rep', 'tp')), may hold values from -0.110485435 to 0.110485435
- weight: bfloat16 [4096, 1024], P(('tp', 'rep')), may hold values from -0.09375 to 0.09375
- momentum: float32 [4096, 1024], P(('tp', 'rep')), may hold values from -3 to 3
Outputs:
- new_weight: bfloat16 [4096, 1024], P(('tp', 'rep'))
- new_momentum: float32 [4096, 1024], P(('tp', 'rep'))
All inputs are finite; a program needn't handle non-finite values.
Results may differ from a plain program's by a relative error of at most 0.0012.
Values may be sent and summed in bfloat16 or wider, within the bound.
A program may use at most 64 MiB of HBM per device.

v0:
```python
import jax
import jax.numpy as jnp
from jax import lax
from jax.sharding import PartitionSpec as P

momentum_decay = 0.9
learning_rate = 0.02


def partner(block, axis, apart):
    count = lax.axis_size(axis)
    route = []
    for low in range(count):
        high = low | 1 << apart
        if high != low and high < count:
            route += [(low, high), (high, low)]
    return lax.ppermute(block, axis, route)


def body(activations, out_grad, weight, momentum):
    row_count = activations.shape[1]
    replicas = lax.axis_size("rep")
    levels = replicas.bit_length() - 1
    rep_index = lax.axis_index("rep")
    piece_rows = row_count // replicas
    current = lax.dot_general(
        activations,
        lax.all_gather(out_grad, "tp", axis=0, tiled=True),
        (((0,), (0,)), ((), ())),
        preferred_element_type=jnp.float32,
    )
    for level in range(levels):
        own_bit = jnp.right_shift(rep_index, level) & 1
        arrived = partner(current, "rep", level)
        lower_part = jnp.where(own_bit == 0, current, arrived)
        upper_part = jnp.where(own_bit == 0, arrived, current)
        partials = jnp.stack(
            [
                jnp.sum(lower_part * upper_part),
                jnp.sum(lower_part * lower_part),
                jnp.sum(upper_part * upper_part),
            ]
        )
        sums = lax.psum(partials, "tp")
        factor_lower = 1.0 - sums[0] / (2.0 * sums[1])
        factor_upper = 1.0 - sums[0] / (2.0 * sums[2])
        current = factor_lower * lower_part + factor_upper * upper_part
    own_rows = lax.dynamic_slice_in_dim(current, rep_index * piece_rows, piece_rows, 0)
    new_momentum = momentum_decay * momentum + own_rows
    new_weight = (weight.astype(jnp.float32) - learning_rate * new_momentum).astype(jnp.bfloat16)
    return (new_weight, new_momentum)


def solution(mesh):
    return jax.shard_map(
        body,
        mesh=mesh,
        in_specs=(
            P("rep", "tp"),
            P(("rep", "tp"), None),
            P(("tp", "rep"), None),
            P(("tp", "rep"), None),
        ),
        out_specs=(P(("tp", "rep"), None), P(("tp", "rep"), None)),
        check_vma=False,
    )
```

profile of v0, /device:TPU:1, one launch (start us, length us, event | category | flops | bytes accessed | tf_op | source)
XLA Modules:
  0.0 420.9 jit_solution(7626095841461541467)
XLA Ops:
  7.9 53.8 %all-gather.2.cloned.1.call-done = bf16[2048,1024]{1,0:T(8,128)(2,1)} async-done(((bf16[128,1024]{1,0:T(8,128)(2,1)}), bf16[2048,1024]{1,0:T(8,128)(2,1)}) %all-gather.2.cloned.1.call-update) | async-done | bytes 4194320 | tf_op jit(solution)/shard_map/all_gather | solution.py:28
  61.8 3.5 fusion.8
  65.2 3.1 collective-permute-start
  68.3 23.4 %collective-permute-done = f32[256,1024]{1,0:T(8,128)} collective-permute-done((f32[256,1024]{1,0:T(8,128)S(1)}, f32[256,1024]{1,0:T(8,128)}, u32[]{:S(2)}, u32[]{:S(2)}) %collective-permute-start) | collective-permute-done | bytes 1048608 | tf_op jit(solution)/shard_map/ppermute | solution.py:17
  91.7 2.5 multiply_reduce_fusion.14
  94.2 2.0 pad_maximum_fusion
  96.2 23.9 %psum.35 = f32[3]{0:T(128)S(1)} all-reduce(f32[3]{0:T(128)S(1)} %pad_maximum_fusion), channel_id=1, replica_groups=mesh['rep'=32,'tp'=16] {'tp'}, use_global_device_ids=true, to_apply=%region_3.4 | all-reduce | flops 3 | bytes 24 | tf_op jit(solution)/shard_map/psum | solution.py:44
  124.7 4.6 %collective-permute-start.1 = (f32[256,1024]{1,0:T(8,128)}, f32[256,1024]{1,0:T(8,128)}, u32[]{:S(2)}, u32[]{:S(2)}) collective-permute-start(f32[256,1024]{1,0:T(8,128)} %multiply_add_fusion.3), channel_id=1, source_target_pairs={{0,32},{32,0},{16,48},{48,16},{64,96},{96,64},{80,112},{112,80},{1... | collective-permute-start | bytes 3145736 | tf_op jit(solution)/shard_map/ppermute | solution.py:17
  129.3 22.6 %collective-permute-done.1 = f32[256,1024]{1,0:T(8,128)} collective-permute-done((f32[256,1024]{1,0:T(8,128)}, f32[256,1024]{1,0:T(8,128)}, u32[]{:S(2)}, u32[]{:S(2)}) %collective-permute-start.1) | collective-permute-done | bytes 1048608 | tf_op jit(solution)/shard_map/ppermute | solution.py:17
  151.9 2.5 multiply_reduce_fusion.11
  156.3 25.0 %psum.36 = f32[3]{0:T(128)S(1)} all-reduce(f32[3]{0:T(128)S(1)} %pad_maximum_fusion.1), channel_id=1, replica_groups=mesh['rep'=32,'tp'=16] {'tp'}, use_global_device_ids=true, to_apply=%region_7.8 | all-reduce | flops 3 | bytes 24 | tf_op jit(solution)/shard_map/psum | solution.py:44
  185.8 3.1 collective-permute-start.2
  188.9 23.1 %collective-permute-done.2 = f32[256,1024]{1,0:T(8,128)} collective-permute-done((f32[256,1024]{1,0:T(8,128)}, f32[256,1024]{1,0:T(8,128)}, u32[]{:S(2)}, u32[]{:S(2)}) %collective-permute-start.2) | collective-permute-done | bytes 1048608 | tf_op jit(solution)/shard_map/ppermute | solution.py:17
  212.1 2.5 multiply_reduce_fusion.8
  216.5 24.4 %psum.37 = f32[3]{0:T(128)S(1)} all-reduce(f32[3]{0:T(128)S(1)} %pad_maximum_fusion.2), channel_id=1, replica_groups=mesh['rep'=32,'tp'=16] {'tp'}, use_global_device_ids=true, to_apply=%region_11.12 | all-reduce | flops 3 | bytes 24 | tf_op jit(solution)/shard_map/psum | solution.py:44
  245.5 4.0 collective-permute-start.3
  249.5 45.7 %collective-permute-done.3 = f32[256,1024]{1,0:T(8,128)} collective-permute-done((f32[256,1024]{1,0:T(8,128)}, f32[256,1024]{1,0:T(8,128)}, u32[]{:S(2)}, u32[]{:S(2)}) %collective-permute-start.3) | collective-permute-done | bytes 1048608 | tf_op jit(solution)/shard_map/ppermute | solution.py:17
  295.2 2.4 multiply_reduce_fusion.5
  297.6 2.0 pad_maximum_fusion.3
  299.6 24.3 %psum.38 = f32[3]{0:T(128)S(1)} all-reduce(f32[3]{0:T(128)S(1)} %pad_maximum_fusion.3), channel_id=1, replica_groups=mesh['rep'=32,'tp'=16] {'tp'}, use_global_device_ids=true, to_apply=%region_15.16 | all-reduce | flops 3 | bytes 24 | tf_op jit(solution)/shard_map/psum | solution.py:44
  328.5 7.1 %collective-permute-start.4 = (f32[256,1024]{1,0:T(8,128)}, f32[256,1024]{1,0:T(8,128)}, u32[]{:S(2)}, u32[]{:S(2)}) collective-permute-start(f32[256,1024]{1,0:T(8,128)} %multiply_add_fusion), channel_id=1, source_target_pairs={{0,256},{256,0},{16,272},{272,16},{32,288},{288,32},{48,304},{304,... | collective-permute-start | bytes 3145736 | tf_op jit(solution)/shard_map/ppermute | solution.py:17
  335.6 45.9 %collective-permute-done.4 = f32[256,1024]{1,0:T(8,128)} collective-permute-done((f32[256,1024]{1,0:T(8,128)}, f32[256,1024]{1,0:T(8,128)}, u32[]{:S(2)}, u32[]{:S(2)}) %collective-permute-start.4) | collective-permute-done | bytes 1048608 | tf_op jit(solution)/shard_map/ppermute | solution.py:17
  381.6 2.4 multiply_reduce_fusion.2
  386.0 24.4 %psum.39 = f32[3]{0:T(128)S(1)} all-reduce(f32[3]{0:T(128)S(1)} %pad_maximum_fusion.4), channel_id=1, replica_groups=mesh['rep'=32,'tp'=16] {'tp'}, use_global_device_ids=true, to_apply=%region_19.20 | all-reduce | flops 3 | bytes 24 | tf_op jit(solution)/shard_map/psum | solution.py:44
  (23 shorter events, 15.3 us)
Async XLA Ops:
  7.2 54.6 %copy-start = (bf16[2048,256]{1,0:T(8,128)(2,1)S(1)}, bf16[2048,256]{1,0:T(8,128)(2,1)}, u32[]{:S(2)}) copy-start(bf16[2048,256]{1,0:T(8,128)(2,1)} %param.4) | copy-start | bytes 3145732
  7.2 54.6 %all-gather.2.cloned.1.call-start = ((), (), s32[]{:S(2)}) async-start(), calls=%async_computation | async-start | bytes 4456448 | tf_op jit(solution)/shard_map/all_gather | solution.py:28
  65.2 3.1 copy-start.1
  65.2 26.5 %collective-permute-start = (f32[256,1024]{1,0:T(8,128)S(1)}, f32[256,1024]{1,0:T(8,128)}, u32[]{:S(2)}, u32[]{:S(2)}) collective-permute-start(f32[256,1024]{1,0:T(8,128)S(1)} %fusion.8), channel_id=1, source_target_pairs={{0,16},{16,0},{32,48},{48,32},{64,80},{80,64},{96,112},{112,96},{1... | collective-permute-start | bytes 3145736 | tf_op jit(solution)/shard_map/ppermute | solution.py:17
  124.7 27.2 %collective-permute-start.1 = (f32[256,1024]{1,0:T(8,128)}, f32[256,1024]{1,0:T(8,128)}, u32[]{:S(2)}, u32[]{:S(2)}) collective-permute-start(f32[256,1024]{1,0:T(8,128)} %multiply_add_fusion.3), channel_id=1, source_target_pairs={{0,32},{32,0},{16,48},{48,16},{64,96},{96,64},{80,112},{112,80},{1... | collective-permute-start | bytes 3145736 | tf_op jit(solution)/shard_map/ppermute | solution.py:17
  185.8 26.3 %collective-permute-start.2 = (f32[256,1024]{1,0:T(8,128)}, f32[256,1024]{1,0:T(8,128)}, u32[]{:S(2)}, u32[]{:S(2)}) collective-permute-start(f32[256,1024]{1,0:T(8,128)} %multiply_add_fusion.2), channel_id=1, source_target_pairs={{0,64},{64,0},{16,80},{80,16},{32,96},{96,32},{48,112},{112,48},{1... | collective-permute-start | bytes 3145736 | tf_op jit(solution)/shard_map/ppermute | solution.py:17
  245.5 49.7 %collective-permute-start.3 = (f32[256,1024]{1,0:T(8,128)}, f32[256,1024]{1,0:T(8,128)}, u32[]{:S(2)}, u32[]{:S(2)}) collective-permute-start(f32[256,1024]{1,0:T(8,128)} %multiply_add_fusion.1), channel_id=1, source_target_pairs={{0,128},{128,0},{16,144},{144,16},{32,160},{160,32},{48,176},{176,... | collective-permute-start | bytes 3145736 | tf_op jit(solution)/shard_map/ppermute | solution.py:17
  297.6 115.8 %copy-start.2 = (f32[8,1024]{1,0:T(8,128)S(1)}, f32[8,1024]{1,0:T(8,128)}, u32[]{:S(2)}) copy-start(f32[8,1024]{1,0:T(8,128)} %param.7) | copy-start | bytes 98308
  297.6 115.8 %copy-start.3 = (bf16[8,1024]{1,0:T(8,128)(2,1)S(1)}, bf16[8,1024]{1,0:T(8,128)(2,1)}, u32[]{:S(2)}) copy-start(bf16[8,1024]{1,0:T(8,128)(2,1)} %param.6) | copy-start | bytes 49156
  328.5 53.0 %collective-permute-start.4 = (f32[256,1024]{1,0:T(8,128)}, f32[256,1024]{1,0:T(8,128)}, u32[]{:S(2)}, u32[]{:S(2)}) collective-permute-start(f32[256,1024]{1,0:T(8,128)} %multiply_add_fusion), channel_id=1, source_target_pairs={{0,256},{256,0},{16,272},{272,16},{32,288},{288,32},{48,304},{304,... | collective-permute-start | bytes 3145736 | tf_op jit(solution)/shard_map/ppermute | solution.py:17
Sparse Core Ops, SparseCore 0:
  10.1 51.5 all-gather.1
where the time goes:
time: 422 us; the launch traced here: 421 us
  waiting for transfers between devices  215 us (51%)
  blocking collectives  122 us (29%)
  other arithmetic  27.6 us (7%)
  between operations  27.3 us (6%)
  starting transfers between devices  21.9 us (5%)
    ppermute x5, waiting for transfers between devices, partner(): return lax.ppermute(block, axis, route)  161 us
    psum x5, blocking collectives, body(): sums = lax.psum(partials, 'tp')  122 us
    all_gather x1, waiting for transfers between devices, body(): lax.all_gather(out_grad, 'tp', axis=0, tiled=True)  53.8 us
    ppermute x5, starting transfers between devices, partner(): return lax.ppermute(block, axis, route)  21.9 us
    reduce_sum x5, other arithmetic, body(): jnp.sum(lower_part * upper_part)  12.3 us
    another operation x5, other arithmetic, body(): jnp.stack([jnp.sum(lower_part * upper_part), jnp.sum(lower_part * lower_p...  9.91 us
  transfers between devices with their start and end apart: 6, of which 6 were waited for; matrix products, arithmetic and copies ran while one was open for 0% of the time, Pallas kernels for 0%

commit v1 on v0

v1 whole, which is shorter than its diff:
```python
import functools

import jax
import jax.numpy as jnp
from jax import lax
from jax.experimental import pallas as pl
from jax.experimental.pallas import tpu as pltpu
from jax.sharding import PartitionSpec as P

MOMENTUM_DECAY = 0.9
LEARNING_RATE = 0.02

NX, NY, NZ = 4, 8, 8
N_REP = NX * NY
N_TP = 2 * NZ
TOKENS = 2048
BLOCK = TOKENS // N_TP
FEATURES = 256
COLUMNS = 1024
ROWS = FEATURES // N_REP
CHUNKS = 8
WIDTH = COLUMNS // CHUNKS
HALF = BLOCK // 2
LANES = 128
FOLD = LANES // N_REP

MESH = pl.DeviceIdType.MESH


def coefficients(gram):
    row = lax.broadcasted_iota(jnp.int32, (N_REP, LANES), 0)
    lane = lax.broadcasted_iota(jnp.int32, (N_REP, LANES), 1)
    column = lane % N_REP
    spread = jnp.broadcast_to(gram[:, None, :], (N_REP // FOLD, FOLD, LANES)).reshape(N_REP, LANES)
    kept = jnp.where(lane // N_REP == row % FOLD, spread, 0.0)
    kept = kept + pltpu.roll(kept, N_REP, 1)
    block = kept + pltpu.roll(kept, 2 * N_REP, 1)
    diagonal = row == column
    weights = jnp.ones((N_REP, LANES), jnp.float32)
    for level in range(N_REP.bit_length() - 1):
        apart = 1 << level
        norm = jnp.sum(jnp.where(diagonal, block, 0.0), axis=0, keepdims=True)
        inner = jnp.sum(jnp.where(row == (column ^ apart), block, 0.0), axis=0, keepdims=True)
        across = jnp.broadcast_to(1.0 - inner / (2.0 * norm), (N_REP, LANES))
        down = jnp.sum(jnp.where(row == lane, across, 0.0), axis=1, keepdims=True)
        down = jnp.broadcast_to(down, (N_REP, LANES))
        weights = weights * down
        block = block * across * down
        upper = (column & apart) != 0
        block = block + jnp.where(
            upper, pltpu.roll(block, apart, 1), pltpu.roll(block, LANES - apart, 1)
        )
        upper = (row & apart) != 0
        block = block + jnp.where(
            upper, pltpu.roll(block, apart, 0), pltpu.roll(block, N_REP - apart, 0)
        )
    return weights


def kernel(
    a_ref, g_ref, w_ref, m_ref, new_w_ref, new_m_ref,
    a_vmem, a_t, gathered, grad, arrived, gram_own, gram_rep, gram_tp, weights, w_vmem, m_vmem,
    load_sem, own_sem, ring_send, ring_recv, pair_send, pair_recv, swap_send, swap_recv,
    gram_send, gram_recv,
):
    rep = lax.axis_index("rep")
    tp = lax.axis_index("tp")
    y, x = rep // NX, lax.rem(rep, NX)
    z, core = tp // 2, lax.rem(tp, 2)
    sibling = z * 2 + (1 - core)
    ahead = lax.rem(z + 1, NZ) * 2 + core
    behind = lax.rem(z + NZ - 1, NZ) * 2 + core

    def remote(src, dst, send_sem, recv_sem, to_rep, to_tp):
        return pltpu.make_async_remote_copy(
            src_ref=src, dst_ref=dst, send_sem=send_sem, recv_sem=recv_sem,
            device_id=(to_rep, to_tp), device_id_type=MESH,
        )

    def rep_peer(step):
        return lax.rem(y + step // NX, NY) * NX + lax.rem(x + lax.rem(step, NX), NX)

    def tp_peer(step):
        return lax.rem(tp + step, N_TP)

    loads = [
        pltpu.make_async_copy(a_ref, a_vmem, load_sem.at[0]),
        pltpu.make_async_copy(w_ref, w_vmem, load_sem.at[1]),
        pltpu.make_async_copy(m_ref, m_vmem, load_sem.at[2]),
    ]
    for copy in loads:
        copy.start()
    own_rows = pl.ds(pl.multiple_of(tp * BLOCK, BLOCK), BLOCK)
    own_copies = [
        pltpu.make_async_copy(
            g_ref.at[:, pl.ds(k * WIDTH, WIDTH)], gathered.at[k, own_rows], own_sem.at[k]
        )
        for k in range(CHUNKS)
    ]
    for copy in own_copies:
        copy.start()

    barrier = pltpu.get_barrier_semaphore()

    @pl.loop(1, N_REP)
    def _(step):
        pl.semaphore_signal(
            barrier, inc=1, device_id=(rep_peer(step), tp), device_id_type=MESH
        )

    @pl.loop(1, N_TP)
    def _(step):
        pl.semaphore_signal(
            barrier, inc=1, device_id=(rep, tp_peer(step)), device_id_type=MESH
        )

    pl.semaphore_wait(barrier, N_REP - 1 + N_TP - 1)

    def rows_from(distance, start=0, size=BLOCK):
        source = lax.rem(z + NZ + distance, NZ) * 2 + core
        return pl.ds(pl.multiple_of(source * BLOCK + start, size), size)

    def ring_step(k, stage):
        for way, to, sign in ((0, ahead, -1), (1, behind, 1)):
            if stage == 0:
                rows = own_rows
                src = g_ref.at[:, pl.ds(k * WIDTH, WIDTH)]
            else:
                if stage < NZ // 2:
                    rows = rows_from(sign * stage)
                else:
                    rows = rows_from(sign * stage, way * HALF, HALF)
                src = gathered.at[k, rows]
                remote(
                    src, src, ring_send.at[k], ring_recv.at[k, way, stage - 1], rep, to
                ).wait_recv()
            if stage < NZ // 2:
                sent_rows, sent = rows, src
                if stage == NZ // 2 - 1:
                    sent_rows = rows_from(sign * stage, way * HALF, HALF)
                    sent = gathered.at[k, sent_rows]
                remote(
                    sent, gathered.at[k, sent_rows], ring_send.at[k],
                    ring_recv.at[k, way, stage], rep, to,
                ).start()
            if stage > 0 or way == 0:
                remote(
                    src, gathered.at[k, rows], pair_send.at[k], pair_recv.at[k], rep, sibling
                ).start()

    def swap_chunk(k):
        own_copies[k].wait()
        half_chunk = gathered.at[k, pl.ds(0, TOKENS // 2)]
        pltpu.make_async_copy(half_chunk, half_chunk, pair_recv.at[k]).wait()
        product = jnp.dot(a_t[...], gathered[k], preferred_element_type=jnp.float32)
        grad[k] = product.reshape(N_REP, ROWS, WIDTH)

        @pl.loop(1, N_REP)
        def _(step):
            peer = rep_peer(step)
            remote(
                grad.at[k, peer], arrived.at[k, rep], swap_send.at[k], swap_recv.at[k], peer, tp
            ).start()

        arrived[k, rep] = grad[k, rep]

    def gram_chunk(k):
        others = arrived.at[k, pl.ds(0, N_REP - 1)]
        pltpu.make_async_copy(others, others, swap_recv.at[k]).wait()
        total = jnp.zeros((N_REP, LANES), jnp.float32)
        for i in range(ROWS):
            part = arrived[k, :, i, :]
            high = part.astype(jnp.bfloat16)
            low = (part - high.astype(jnp.float32)).astype(jnp.bfloat16)
            high_all = jnp.concatenate([high] * FOLD, axis=0)
            low_all = jnp.concatenate([low] * FOLD, axis=0)
            for left, right in ((high, high_all), (high, low_all), (low, high_all)):
                total += lax.dot_general(
                    left, right, (((1,), (1,)), ((), ())), preferred_element_type=jnp.float32
                )
        return total

    for k in range(0, CHUNKS):
        pass

    gram = jnp.zeros((N_REP, LANES), jnp.float32)
    rounds = CHUNKS + NZ // 2 + 1
    for j in range(rounds):
        if j == 1:
            loads[0].wait()
            for i in range(TOKENS // FEATURES):
                span = pl.ds(i * FEATURES, FEATURES)
                a_t[:, span] = a_vmem[span, :].T
        for stage in range(NZ // 2, -1, -1):
            k = j - stage
            if 0 <= k < CHUNKS:
                ring_step(k, stage)
        k = j - NZ // 2
        if 0 <= k < CHUNKS:
            swap_chunk(k)
        if 0 <= k - 1 < CHUNKS:
            gram += gram_chunk(k - 1)

    row = lax.broadcasted_iota(jnp.int32, (N_REP, LANES), 0)
    lane = lax.broadcasted_iota(jnp.int32, (N_REP, LANES), 1)
    folded = jnp.where(lane // N_REP == row % FOLD, gram, 0.0)
    folded = jnp.sum(folded.reshape(N_REP // FOLD, FOLD, LANES), axis=1)

    gram_own[0] = folded

    @pl.loop(1, N_TP)
    def _(step):
        remote(
            gram_own.at[0], gram_tp.at[tp], gram_send.at[0], gram_recv.at[0], rep, tp_peer(step)
        ).start()

    gram_tp[tp] = folded
    others = gram_tp.at[pl.ds(0, N_TP - 1)]
    pltpu.make_async_copy(others, others, gram_recv.at[0]).wait()
    replica_sum = jnp.sum(gram_tp[...], axis=0)
    gram_own[1] = replica_sum

    @pl.loop(1, N_REP)
    def _(step):
        remote(
            gram_own.at[1], gram_rep.at[rep], gram_send.at[1], gram_recv.at[1], rep_peer(step), tp
        ).start()

    gram_rep[rep] = replica_sum
    others = gram_rep.at[pl.ds(0, N_REP - 1)]
    pltpu.make_async_copy(others, others, gram_recv.at[1]).wait()
    weights[...] = coefficients(jnp.sum(gram_rep[...], axis=0))

    loads[1].wait()
    loads[2].wait()
    for k in range(CHUNKS):
        span = pl.ds(k * WIDTH, WIDTH)
        combined = jnp.zeros((ROWS, WIDTH), jnp.float32)
        for r in range(N_REP):
            combined += weights[pl.ds(r, 1), pl.ds(0, WIDTH)] * arrived[k, r]
        new_m = MOMENTUM_DECAY * m_vmem[:, span] + combined
        new_m_ref[:, span] = new_m
        new_w = w_vmem[:, span].astype(jnp.float32) - LEARNING_RATE * new_m
        new_w_ref[:, span] = new_w.astype(jnp.bfloat16)

    for k in range(CHUNKS):
        sent = gathered.at[k, pl.ds(0, 7 * BLOCK)]
        pltpu.make_async_copy(sent, sent, ring_send.at[k]).wait()
        sent = gathered.at[k, pl.ds(0, 8 * BLOCK)]
        pltpu.make_async_copy(sent, sent, pair_send.at[k]).wait()
        sent = grad.at[k, pl.ds(0, N_REP - 1)]
        pltpu.make_async_copy(sent, sent, swap_send.at[k]).wait()
    sent = gram_tp.at[pl.ds(0, N_TP - 1)]
    pltpu.make_async_copy(sent, sent, gram_send.at[0]).wait()
    sent = gram_rep.at[pl.ds(0, N_REP - 1)]
    pltpu.make_async_copy(sent, sent, gram_send.at[1]).wait()


def body(activations, out_grad, weight, momentum):
    dma = pltpu.SemaphoreType.DMA
    return pl.pallas_call(
        kernel,
        out_shape=(
            jax.ShapeDtypeStruct(weight.shape, jnp.bfloat16),
            jax.ShapeDtypeStruct(momentum.shape, jnp.float32),
        ),
        in_specs=[pl.BlockSpec(memory_space=pl.ANY)] * 4,
        out_specs=(pl.BlockSpec(memory_space=pltpu.VMEM),) * 2,
        scratch_shapes=[
            pltpu.VMEM((TOKENS, FEATURES), jnp.bfloat16),
            pltpu.VMEM((FEATURES, TOKENS), jnp.bfloat16),
            pltpu.VMEM((CHUNKS, TOKENS, WIDTH), jnp.bfloat16),
            pltpu.VMEM((CHUNKS, N_REP, ROWS, WIDTH), jnp.float32),
            pltpu.VMEM((CHUNKS, N_REP, ROWS, WIDTH), jnp.float32),
            pltpu.VMEM((2, ROWS, LANES), jnp.float32),
            pltpu.VMEM((N_REP, ROWS, LANES), jnp.float32),
            pltpu.VMEM((N_TP, ROWS, LANES), jnp.float32),
            pltpu.VMEM((N_REP, LANES), jnp.float32),
            pltpu.VMEM((ROWS, COLUMNS), jnp.bfloat16),
            pltpu.VMEM((ROWS, COLUMNS), jnp.float32),
            dma((3,)),
            dma((CHUNKS,)),
            dma((CHUNKS,)),
            dma((CHUNKS, 2, NZ // 2)),
            dma((CHUNKS,)),
            dma((CHUNKS,)),
            dma((CHUNKS,)),
            dma((CHUNKS,)),
            dma((2,)),
            dma((2,)),
        ],
        compiler_params=pltpu.CompilerParams(
            collective_id=0, has_side_effects=True, vmem_limit_bytes=48 * 1024 * 1024
        ),
    )(activations, out_grad, weight, momentum)


def solution(mesh):
    return jax.shard_map(
        body,
        mesh=mesh,
        in_specs=(
            P("rep", "tp"),
            P(("rep", "tp"), None),
            P(("tp", "rep"), None),
            P(("tp", "rep"), None),
        ),
        out_specs=(P(("tp", "rep"), None), P(("tp", "rep"), None)),
        check_vma=False,
    )
```

time: 422 us -> 96.2 us (0.23)
  waiting for transfers between devices: 215 us -> 0 us
  blocking collectives: 122 us -> 0 us
  Pallas kernels: 0 us -> 90.4 us
  other arithmetic: 27.6 us -> 0 us
  between operations: 27.3 us -> 0.65 us
  starting transfers between devices: 21.9 us -> 0 us
    ppermute x5 -> x0, waiting for transfers between devices: 161 us -> none  [partner(): return lax.ppermute(block, axis, route)]
    psum x5 -> x0, blocking collectives: 122 us -> none  [body(): sums = lax.psum(partials, 'tp')]
    pallas_call x0 -> x1, Pallas kernels: none -> 90.4 us  [body(): pl.pallas_call(kernel, out_shape=(jax.ShapeDtypeStruct(weight.shape, jnp....]
    all_gather x1 -> x0, waiting for transfers between devices: 53.8 us -> none  [body(): lax.all_gather(out_grad, 'tp', axis=0, tiled=True)]
    ppermute x5 -> x0, starting transfers between devices: 21.9 us -> none  [partner(): return lax.ppermute(block, axis, route)]
    reduce_sum x5 -> x0, other arithmetic: 12.3 us -> none  [body(): jnp.sum(lower_part * upper_part)]
    another operation x5 -> x0, other arithmetic: 9.91 us -> none  [body(): jnp.stack([jnp.sum(lower_part * upper_part), jnp.sum(lower_part * lower_p...]
    unnamed x8 -> x10, local copies, waits for them, and re-layouts: 0.02 us -> 4.86 us
  transfers between devices with their start and end apart: 6 -> 0, of which waited for: 6 -> 0; matrix products, arithmetic and copies ran while one was open for 0% -> 0% of each run, Pallas kernels for 0% -> 0%
where the time goes in v1:
time: 96.2 us; the launch traced here: 95.9 us
  Pallas kernels  90.4 us (94%)
  local copies, waits for them, and re-layouts  4.86 us (5%)
    pallas_call x1, Pallas kernels, body(): pl.pallas_call(kernel, out_shape=(jax.ShapeDtypeStruct(weight.shape, jnp....  90.4 us
    unnamed x10, local copies, waits for them, and re-layouts  4.86 us

profile of v1, /device:TPU:1, one launch (start us, length us, event | category | flops | bytes accessed | tf_op | source)
XLA Modules:
  0.0 95.9 jit_solution(12377107761263234622)
XLA Ops:
  0.6 0.0 copy-start
  0.6 1.2 %copy-done = bf16[2048,256]{1,0:T(8,128)(2,1)S(1)} copy-done((bf16[2048,256]{1,0:T(8,128)(2,1)S(1)}, bf16[2048,256]{1,0:T(8,128)(2,1)}, u32[]{:S(2)}) %copy-start) | copy-done | bytes 1048600
  1.9 0.0 copy-start.1
  1.9 0.9 copy-done.1
  2.8 0.0 copy-start.2
  2.8 0.8 copy-done.2
  3.6 0.0 copy-start.3
  3.6 0.7 copy-done.3
  4.3 90.4 %shard_map.59 = (bf16[8,1024]{1,0:T(8,128)(2,1)S(1)}, f32[8,1024]{1,0:T(8,128)S(1)}) custom-call(bf16[2048,256]{1,0:T(8,128)(2,1)S(1)} %copy-done, bf16[128,1024]{1,0:T(8,128)(2,1)S(1)} %copy-done.1, bf16[8,1024]{1,0:T(8,128)(2,1)S(1)} %copy-done.3, f32[8,1024]{1,0:T(8,128)S(1)} %copy-done.2), custom_call_target="tpu_custom_call" | custom-call | tf_op jit(solution)/shard_map/pallas_call | solution.py:261
  94.7 0.6 copy.8
  95.3 0.6 copy.9
Async XLA Ops:
  0.6 1.2 %copy-start = (bf16[2048,256]{1,0:T(8,128)(2,1)S(1)}, bf16[2048,256]{1,0:T(8,128)(2,1)}, u32[]{:S(2)}) copy-start(bf16[2048,256]{1,0:T(8,128)(2,1)} %a_ref.1) | copy-start | bytes 3145732
  1.9 0.9 copy-start.1
  2.8 0.8 copy-start.2
  3.6 0.7 copy-start.3

commit v2 on v1

v2 whole, which is shorter than its diff:
```python
import functools

import jax
import jax.numpy as jnp
from jax import lax
from jax.experimental import pallas as pl
from jax.experimental.pallas import tpu as pltpu
from jax.sharding import PartitionSpec as P

MOMENTUM_DECAY = 0.9
LEARNING_RATE = 0.02

NX, NY, NZ = 4, 8, 8
N_REP = NX * NY
N_TP = 2 * NZ
TOKENS = 2048
BLOCK = TOKENS // N_TP
FEATURES = 256
COLUMNS = 1024
ROWS = FEATURES // N_REP
CHUNKS = 4
WIDTH = COLUMNS // CHUNKS
HALF = BLOCK // 2
LANES = 128
FOLD = LANES // N_REP
PARTS = WIDTH // LANES
PACKED = ROWS * PARTS
GAP = 3
LOW_AFTER = 2

MESH = pl.DeviceIdType.MESH


def ring_order():
    sent, order, slot = [[] for _ in range(CHUNKS)], [], 0.0
    while len(order) < CHUNKS * (NZ // 2 + 1):
        for k in range(CHUNKS):
            stage = len(sent[k])
            if stage <= NZ // 2 and (stage == 0 or sent[k][-1] + GAP <= slot):
                sent[k].append(slot)
                order.append((k, stage))
                if stage < NZ // 2:
                    slot += 0.5 if stage == NZ // 2 - 1 else 1.0
                break
        else:
            slot += 0.5
    return order


def coefficients(gram):
    row = lax.broadcasted_iota(jnp.int32, (N_REP, LANES), 0)
    lane = lax.broadcasted_iota(jnp.int32, (N_REP, LANES), 1)
    column = lane % N_REP
    spread = jnp.broadcast_to(gram[:, None, :], (N_REP // FOLD, FOLD, LANES)).reshape(N_REP, LANES)
    kept = jnp.where(lane // N_REP == row % FOLD, spread, 0.0)
    kept = kept + pltpu.roll(kept, N_REP, 1)
    block = kept + pltpu.roll(kept, 2 * N_REP, 1)
    diagonal = row == column
    weights = jnp.ones((N_REP, LANES), jnp.float32)
    for level in range(N_REP.bit_length() - 1):
        apart = 1 << level
        norm = jnp.sum(jnp.where(diagonal, block, 0.0), axis=0, keepdims=True)
        inner = jnp.sum(jnp.where(row == (column ^ apart), block, 0.0), axis=0, keepdims=True)
        across = jnp.broadcast_to(1.0 - inner / (2.0 * norm), (N_REP, LANES))
        down = jnp.sum(jnp.where(row == lane, across, 0.0), axis=1, keepdims=True)
        down = jnp.broadcast_to(down, (N_REP, LANES))
        weights = weights * down
        block = block * across * down
        upper = (column & apart) != 0
        block = block + jnp.where(
            upper, pltpu.roll(block, apart, 1), pltpu.roll(block, LANES - apart, 1)
        )
        upper = (row & apart) != 0
        block = block + jnp.where(
            upper, pltpu.roll(block, apart, 0), pltpu.roll(block, N_REP - apart, 0)
        )
    return weights


def kernel(
    a_ref, g_ref, w_ref, m_ref, new_w_ref, new_m_ref,
    a_vmem, a_t, gathered, high_own, low_own, high_in, low_in, full,
    gram_own, gram_rep, gram_tp, weights, w_vmem, m_vmem,
    load_sem, own_sem, ring_send, ring_recv, pair_send, pair_recv, high_send, high_recv,
    low_send, low_recv, gram_send, gram_recv,
):
    rep = lax.axis_index("rep")
    tp = lax.axis_index("tp")
    y, x = rep // NX, lax.rem(rep, NX)
    z, core = tp // 2, lax.rem(tp, 2)
    sibling = z * 2 + (1 - core)
    ahead = lax.rem(z + 1, NZ) * 2 + core
    behind = lax.rem(z + NZ - 1, NZ) * 2 + core
    in_x = [lax.rem(x + d, NX) for d in range(NX)]
    far_x = sorted(range(NX), key=lambda d: -min(d, NX - d))
    far_y = sorted(range(NY), key=lambda d: -min(d, NY - d))
    far_z = sorted(range(NZ), key=lambda d: -min(d, NZ - d))
    in_y = [lax.rem(y + d, NY) * NX for d in range(NY)]
    rep_peers = [in_y[dy] + in_x[dx] for dy in far_y for dx in far_x if dy or dx]
    in_z = [lax.rem(z + d, NZ) * 2 for d in range(NZ)]
    tp_peers = [in_z[dz] + (core if same else 1 - core) for dz in far_z for same in (0, 1) if dz or not same]

    def remote(src, dst, send_sem, recv_sem, to_rep, to_tp):
        return pltpu.make_async_remote_copy(
            src_ref=src, dst_ref=dst, send_sem=send_sem, recv_sem=recv_sem,
            device_id=(to_rep, to_tp), device_id_type=MESH,
        )

    def wait_bytes(ref, sem):
        pltpu.make_async_copy(ref, ref, sem).wait()

    loads = [
        pltpu.make_async_copy(a_ref, a_vmem, load_sem.at[0]),
        pltpu.make_async_copy(w_ref, w_vmem, load_sem.at[1]),
        pltpu.make_async_copy(m_ref, m_vmem, load_sem.at[2]),
    ]
    own_rows = pl.ds(pl.multiple_of(tp * BLOCK, BLOCK), BLOCK)
    own_copies = [
        pltpu.make_async_copy(
            g_ref.at[:, pl.ds(k * WIDTH, WIDTH)], gathered.at[k, own_rows], own_sem.at[k]
        )
        for k in range(CHUNKS)
    ]

    barrier = pltpu.get_barrier_semaphore()
    for peer in tp_peers[::-1]:
        pl.semaphore_signal(barrier, inc=1, device_id=(rep, peer), device_id_type=MESH)
    for peer in rep_peers:
        pl.semaphore_signal(barrier, inc=1, device_id=(peer, tp), device_id_type=MESH)
    for copy in loads + own_copies:
        copy.start()
    loads[0].wait()
    for i in range(TOKENS // FEATURES):
        span = pl.ds(i * FEATURES, FEATURES)
        a_t[:, span] = a_vmem[span, :].T
    pl.semaphore_wait(barrier, N_REP - 1 + N_TP - 1)

    def rows_from(distance, start=0, size=BLOCK):
        source = lax.rem(z + NZ + distance, NZ) * 2 + core
        return pl.ds(pl.multiple_of(source * BLOCK + start, size), size)

    def ring_step(k, stage):
        for way, to, sign in ((0, ahead, -1), (1, behind, 1)):
            if stage == 0:
                rows = own_rows
                src = g_ref.at[:, pl.ds(k * WIDTH, WIDTH)]
            else:
                if stage < NZ // 2:
                    rows = rows_from(sign * stage)
                else:
                    rows = rows_from(sign * stage, way * HALF, HALF)
                src = gathered.at[k, rows]
                remote(
                    src, src, ring_send.at[k], ring_recv.at[k, way, stage - 1], rep, to
                ).wait_recv()
            if stage < NZ // 2:
                sent_rows, sent = rows, src
                if stage == NZ // 2 - 1:
                    sent_rows = rows_from(sign * stage, way * HALF, HALF)
                    sent = gathered.at[k, sent_rows]
                remote(
                    sent, gathered.at[k, sent_rows], ring_send.at[k],
                    ring_recv.at[k, way, stage], rep, to,
                ).start()
            if stage > 0 or way == 0:
                remote(
                    src, gathered.at[k, rows], pair_send.at[k], pair_recv.at[k], rep, sibling
                ).start()

    def send_rows(own, into, send_sem, recv_sem, k):
        def to(peer):
            remote(
                own.at[k, peer], into.at[k, rep], send_sem.at[k], recv_sem.at[k], peer, tp
            ).start()

        def to_row(dy):
            row = lax.rem(y + dy, NY) * NX
            for dx in far_x:
                to(row + in_x[dx])

        to_row(NY // 2)

        @pl.loop(1, NY // 2)
        def _(step):
            to_row(NY // 2 - step)
            to_row(NY // 2 + step)

        for dx in far_x:
            if dx:
                to(y * NX + in_x[dx])
        into[k, rep] = own[k, rep]

    def send_high(k):
        own_copies[k].wait()
        wait_bytes(gathered.at[k, pl.ds(0, TOKENS // 2)], pair_recv.at[k])
        product = jnp.dot(a_t[...], gathered[k], preferred_element_type=jnp.float32)
        product = jnp.concatenate(
            [
                product[:, p * LANES:(p + 1) * LANES].reshape(N_REP, ROWS, LANES)
                for p in range(PARTS)
            ],
            axis=1,
        )
        high = product.astype(jnp.bfloat16)
        high_own[k] = high
        send_rows(high_own, high_in, high_send, high_recv, k)
        low_own[k] = (product - high.astype(jnp.float32)).astype(jnp.bfloat16)

    def send_low(k):
        send_rows(low_own, low_in, low_send, low_recv, k)

    def gram_chunk(k):
        wait_bytes(high_in.at[k, pl.ds(0, N_REP - 1)], high_recv.at[k])
        full[k] = high_in[k].astype(jnp.float32)
        total = jnp.zeros((N_REP, LANES), jnp.float32)
        for i in range(0, PACKED, 2):
            part = jnp.concatenate([full[k, :, i, :], full[k, :, i + 1, :]], axis=1)
            part = part.astype(jnp.bfloat16)
            total += lax.dot_general(
                part, jnp.concatenate([part] * FOLD, axis=0),
                (((1,), (1,)), ((), ())), preferred_element_type=jnp.float32,
            )
        return total

    done = 0
    for k, stage in ring_order():
        ring_step(k, stage)
        if stage == NZ // 2:
            send_high(k)
            done += 1
            if done < CHUNKS and done - LOW_AFTER >= 0:
                send_low(done - LOW_AFTER)
    lows = [k for k in range(CHUNKS) if not (LOW_AFTER <= k + LOW_AFTER < CHUNKS)]
    for k in lows:
        send_low(k)

    gram = jnp.zeros((N_REP, LANES), jnp.float32)
    for k in range(CHUNKS):
        gram += gram_chunk(k)

    row = lax.broadcasted_iota(jnp.int32, (N_REP, LANES), 0)
    lane = lax.broadcasted_iota(jnp.int32, (N_REP, LANES), 1)
    folded = jnp.where(lane // N_REP == row % FOLD, gram, 0.0)
    folded = jnp.sum(folded.reshape(N_REP // FOLD, FOLD, LANES), axis=1)

    gram_own[0] = folded
    for peer in tp_peers:
        remote(
            gram_own.at[0], gram_tp.at[tp], gram_send.at[0], gram_recv.at[0], rep, peer
        ).start()
    gram_tp[tp] = folded
    wait_bytes(gram_tp.at[pl.ds(0, N_TP - 1)], gram_recv.at[0])
    replica_sum = jnp.sum(gram_tp[...], axis=0)
    gram_own[1] = replica_sum
    for peer in rep_peers:
        remote(
            gram_own.at[1], gram_rep.at[rep], gram_send.at[1], gram_recv.at[1], peer, tp
        ).start()
    gram_rep[rep] = replica_sum

    for k in range(CHUNKS):
        wait_bytes(low_in.at[k, pl.ds(0, N_REP - 1)], low_recv.at[k])
        full[k] += low_in[k].astype(jnp.float32)
    loads[1].wait()
    loads[2].wait()
    for k in range(CHUNKS):
        wait_bytes(gathered.at[k, pl.ds(0, 7 * BLOCK)], ring_send.at[k])
        wait_bytes(gathered.at[k, pl.ds(0, 8 * BLOCK)], pair_send.at[k])
        wait_bytes(high_own.at[k, pl.ds(0, N_REP - 1)], high_send.at[k])
        wait_bytes(low_own.at[k, pl.ds(0, N_REP - 1)], low_send.at[k])
    wait_bytes(gram_tp.at[pl.ds(0, N_TP - 1)], gram_send.at[0])

    wait_bytes(gram_rep.at[pl.ds(0, N_REP - 1)], gram_recv.at[1])
    weights[...] = coefficients(jnp.sum(gram_rep[...], axis=0))
    for k in range(CHUNKS):
        combined = jnp.zeros((PACKED, LANES), jnp.float32)
        for r in range(N_REP):
            combined += weights[pl.ds(r, 1), :] * full[k, r]
        for p in range(PARTS):
            span = pl.ds(k * WIDTH + p * LANES, LANES)
            new_m = MOMENTUM_DECAY * m_vmem[:, span] + combined[p * ROWS:(p + 1) * ROWS]
            new_m_ref[:, span] = new_m
            new_w = w_vmem[:, span].astype(jnp.float32) - LEARNING_RATE * new_m
            new_w_ref[:, span] = new_w.astype(jnp.bfloat16)
    wait_bytes(gram_rep.at[pl.ds(0, N_REP - 1)], gram_send.at[1])


def body(activations, out_grad, weight, momentum):
    dma = pltpu.SemaphoreType.DMA
    return pl.pallas_call(
        kernel,
        out_shape=(
            jax.ShapeDtypeStruct(weight.shape, jnp.bfloat16),
            jax.ShapeDtypeStruct(momentum.shape, jnp.float32),
        ),
        in_specs=[pl.BlockSpec(memory_space=pltpu.HBM)] * 4,
        out_specs=(pl.BlockSpec(memory_space=pltpu.VMEM),) * 2,
        scratch_shapes=[
            pltpu.VMEM((TOKENS, FEATURES), jnp.bfloat16),
            pltpu.VMEM((FEATURES, TOKENS), jnp.bfloat16),
            pltpu.VMEM((CHUNKS, TOKENS, WIDTH), jnp.bfloat16),
            pltpu.VMEM((CHUNKS, N_REP, PACKED, LANES), jnp.bfloat16),
            pltpu.VMEM((CHUNKS, N_REP, PACKED, LANES), jnp.bfloat16),
            pltpu.VMEM((CHUNKS, N_REP, PACKED, LANES), jnp.bfloat16),
            pltpu.VMEM((CHUNKS, N_REP, PACKED, LANES), jnp.bfloat16),
            pltpu.VMEM((CHUNKS, N_REP, PACKED, LANES), jnp.float32),
            pltpu.VMEM((2, ROWS, LANES), jnp.float32),
            pltpu.VMEM((N_REP, ROWS, LANES), jnp.float32),
            pltpu.VMEM((N_TP, ROWS, LANES), jnp.float32),
            pltpu.VMEM((N_REP, LANES), jnp.float32),
            pltpu.VMEM((ROWS, COLUMNS), jnp.bfloat16),
            pltpu.VMEM((ROWS, COLUMNS), jnp.float32),
            dma((3,)),
            dma((CHUNKS,)),
            dma((CHUNKS,)),
            dma((CHUNKS, 2, NZ // 2)),
            dma((CHUNKS,)),
            dma((CHUNKS,)),
            dma((CHUNKS,)),
            dma((CHUNKS,)),
            dma((CHUNKS,)),
            dma((CHUNKS,)),
            dma((2,)),
            dma((2,)),
        ],
        compiler_params=pltpu.CompilerParams(
            collective_id=0, has_side_effects=True, vmem_limit_bytes=62 * 1024 * 1024
        ),
    )(activations, out_grad, weight, momentum)


def solution(mesh):
    return jax.shard_map(
        body,
        mesh=mesh,
        in_specs=(
            P("rep", "tp"),
            P(("rep", "tp"), None),
            P(("tp", "rep"), None),
            P(("tp", "rep"), None),
        ),
        out_specs=(P(("tp", "rep"), None), P(("tp", "rep"), None)),
        check_vma=False,
    )
```

time: 96.2 us -> 71.8 us (0.75)
  Pallas kernels: 90.4 us -> 69 us
  local copies, waits for them, and re-layouts: 4.86 us -> 1.95 us
    pallas_call x1, Pallas kernels: 90.4 us -> 69 us  [body(): pl.pallas_call(kernel, out_shape=(jax.ShapeDtypeStruct(weight.shape, jnp....]
    unnamed x10 -> x4, local copies, waits for them, and re-layouts: 4.86 us -> 1.95 us
where the time goes in v2:
time: 71.8 us; the launch traced here: 71.5 us
  Pallas kernels  69 us (96%)
  local copies, waits for them, and re-layouts  1.95 us (3%)
    pallas_call x1, Pallas kernels, body(): pl.pallas_call(kernel, out_shape=(jax.ShapeDtypeStruct(weight.shape, jnp....  69 us
    unnamed x4, local copies, waits for them, and re-layouts  1.95 us

profile of v2, /device:TPU:1, one launch (start us, length us, event | category | flops | bytes accessed | tf_op | source)
XLA Modules:
  0.0 71.5 jit_solution(16839776306858975533)
XLA Ops:
  0.6 69.0 %shard_map.59 = (bf16[8,1024]{1,0:T(8,128)(2,1)}, f32[8,1024]{1,0:T(8,128)}) custom-call(bf16[2048,256]{1,0:T(8,128)(2,1)} %a_ref.1, bf16[128,1024]{1,0:T(8,128)(2,1)} %g_ref.1, bf16[8,1024]{1,0:T(8,128)(2,1)} %w_ref.1, f32[8,1024]{1,0:T(8,128)} %m_ref.1), custom_call_target="tpu_custom_call" | custom-call | tf_op jit(solution)/shard_map/pallas_call | solution.py:290
  69.6 0.0 copy-start
  69.6 1.3 %copy.8 = bf16[8,1024]{1,0:T(8,128)(2,1)} copy(bf16[8,1024]{1,0:T(8,128)(2,1)} %get-tuple-element.4) | data formatting | bytes 32768
  70.9 0.0 copy-done
  70.9 0.6 copy.9
Async XLA Ops:
  69.6 1.3 %copy-start = (f32[8,1024]{1,0:T(8,128)S(1)}, f32[8,1024]{1,0:T(8,128)}, u32[]{:S(2)}) copy-start(f32[8,1024]{1,0:T(8,128)} %get-tuple-element.5) | copy-start | bytes 98308

commit v3 on v2

--- a/solution.py
+++ b/solution.py
@@ -25,26 +25,18 @@
 FOLD = LANES // N_REP
 PARTS = WIDTH // LANES
 PACKED = ROWS * PARTS
-GAP = 3
-LOW_AFTER = 2
 
 MESH = pl.DeviceIdType.MESH
 
 
-def ring_order():
-    sent, order, slot = [[] for _ in range(CHUNKS)], [], 0.0
-    while len(order) < CHUNKS * (NZ // 2 + 1):
-        for k in range(CHUNKS):
-            stage = len(sent[k])
-            if stage <= NZ // 2 and (stage == 0 or sent[k][-1] + GAP <= slot):
-                sent[k].append(slot)
-                order.append((k, stage))
-                if stage < NZ // 2:
-                    slot += 0.5 if stage == NZ // 2 - 1 else 1.0
-                break
-        else:
-            slot += 0.5
-    return order
+ORDER = (
+    (0, 0), (1, 0), (2, 0), (0, 1), (3, 0), (1, 1), (0, 2), (2, 1), (1, 2), (0, 3),
+    (3, 1), (2, 2), (1, 3), (0, 4), (3, 2), (2, 3), (1, 4), (3, 3), (2, 4), (3, 4),
+)
+EARLY_LOW = {0: 0}
+MID_LOW = (1, 2, 3)
+LATE_LOW = ()
+GREET = {4: 0, 7: 1, 10: 2, 12: 3}
 
 
 def coefficients(gram):
@@ -82,7 +74,7 @@
     a_vmem, a_t, gathered, high_own, low_own, high_in, low_in, full,
     gram_own, gram_rep, gram_tp, weights, w_vmem, m_vmem,
     load_sem, own_sem, ring_send, ring_recv, pair_send, pair_recv, high_send, high_recv,
-    low_send, low_recv, gram_send, gram_recv,
+    low_send, low_recv, gram_send, gram_recv, greet_sem,
 ):
     rep = lax.axis_index("rep")
     tp = lax.axis_index("tp")
@@ -123,17 +115,25 @@
     ]
 
     barrier = pltpu.get_barrier_semaphore()
-    for peer in tp_peers[::-1]:
+    for peer in (sibling, ahead, behind):
         pl.semaphore_signal(barrier, inc=1, device_id=(rep, peer), device_id_type=MESH)
-    for peer in rep_peers:
+    for peer in [in_y[0] + in_x[d] for d in range(1, NX)] + [in_y[d] + x for d in (1, NY - 1)]:
         pl.semaphore_signal(barrier, inc=1, device_id=(peer, tp), device_id_type=MESH)
+
+    def greet(turn):
+        for d in (1, NY - 1):
+            pl.semaphore_signal(
+                greet_sem.at[turn], inc=1, device_id=(in_y[d] + x, tp), device_id_type=MESH
+            )
+
     for copy in loads + own_copies:
         copy.start()
     loads[0].wait()
     for i in range(TOKENS // FEATURES):
         span = pl.ds(i * FEATURES, FEATURES)
         a_t[:, span] = a_vmem[span, :].T
-    pl.semaphore_wait(barrier, N_REP - 1 + N_TP - 1)
+    pl.semaphore_wait(barrier, 3 + NX - 1 + 2)
+    greet(0)
 
     def rows_from(distance, start=0, size=BLOCK):
         source = lax.rem(z + NZ + distance, NZ) * 2 + core
@@ -222,16 +222,18 @@
             )
         return total
 
-    done = 0
-    for k, stage in ring_order():
+    for i, (k, stage) in enumerate(ORDER):
+        if i in GREET:
+            turn = GREET[i]
+            pl.semaphore_wait(greet_sem.at[turn], 2)
+            if turn + 1 < NY // 2:
+                greet(turn + 1)
         ring_step(k, stage)
         if stage == NZ // 2:
             send_high(k)
-            done += 1
-            if done < CHUNKS and done - LOW_AFTER >= 0:
-                send_low(done - LOW_AFTER)
-    lows = [k for k in range(CHUNKS) if not (LOW_AFTER <= k + LOW_AFTER < CHUNKS)]
-    for k in lows:
+            if k in EARLY_LOW:
+                send_low(EARLY_LOW[k])
+    for k in MID_LOW:
         send_low(k)
 
     gram = jnp.zeros((N_REP, LANES), jnp.float32)
@@ -248,6 +250,8 @@
         remote(
             gram_own.at[0], gram_tp.at[tp], gram_send.at[0], gram_recv.at[0], rep, peer
         ).start()
+    for k in LATE_LOW:
+        send_low(k)
     gram_tp[tp] = folded
     wait_bytes(gram_tp.at[pl.ds(0, N_TP - 1)], gram_recv.at[0])
     replica_sum = jnp.sum(gram_tp[...], axis=0)
@@ -322,6 +326,7 @@
             dma((CHUNKS,)),
             dma((2,)),
             dma((2,)),
+            pltpu.SemaphoreType.REGULAR((NY // 2,)),
         ],
         compiler_params=pltpu.CompilerParams(
             collective_id=0, has_side_effects=True, vmem_limit_bytes=62 * 1024 * 1024

time: 71.8 us -> 65.6 us (0.914)
  Pallas kernels: 69 us -> 62.8 us
    pallas_call x1, Pallas kernels: 69 us -> 62.8 us  [body(): pl.pallas_call(kernel, out_shape=(jax.ShapeDtypeStruct(weight.shape, jnp....]
where the time goes in v3:
time: 65.6 us; the launch traced here: 65.3 us
  Pallas kernels  62.8 us (96%)
  local copies, waits for them, and re-layouts  1.95 us (3%)
    pallas_call x1, Pallas kernels, body(): pl.pallas_call(kernel, out_shape=(jax.ShapeDtypeStruct(weight.shape, jnp....  62.8 us
    unnamed x4, local copies, waits for them, and re-layouts  1.95 us

profile of v3, /device:TPU:1, one launch (start us, length us, event | category | flops | bytes accessed | tf_op | source)
XLA Modules:
  0.0 65.3 jit_solution(16353857238800488213)
XLA Ops:
  0.6 62.8 %shard_map.59 = (bf16[8,1024]{1,0:T(8,128)(2,1)}, f32[8,1024]{1,0:T(8,128)}) custom-call(bf16[2048,256]{1,0:T(8,128)(2,1)} %a_ref.1, bf16[128,1024]{1,0:T(8,128)(2,1)} %g_ref.1, bf16[8,1024]{1,0:T(8,128)(2,1)} %w_ref.1, f32[8,1024]{1,0:T(8,128)} %m_ref.1), custom_call_target="tpu_custom_call" | custom-call | tf_op jit(solution)/shard_map/pallas_call | solution.py:294
  63.4 0.0 copy-start
  63.4 1.3 %copy.8 = bf16[8,1024]{1,0:T(8,128)(2,1)} copy(bf16[8,1024]{1,0:T(8,128)(2,1)} %get-tuple-element.4) | data formatting | bytes 32768
  64.7 0.0 copy-done
  64.7 0.6 copy.9
Async XLA Ops:
  63.4 1.3 %copy-start = (f32[8,1024]{1,0:T(8,128)S(1)}, f32[8,1024]{1,0:T(8,128)}, u32[]{:S(2)}) copy-start(f32[8,1024]{1,0:T(8,128)} %get-tuple-element.5) | copy-start | bytes 98308

commit v4 on v3

--- a/solution.py
+++ b/solution.py
@@ -33,6 +33,8 @@
     (0, 0), (1, 0), (2, 0), (0, 1), (3, 0), (1, 1), (0, 2), (2, 1), (1, 2), (0, 3),
     (3, 1), (2, 2), (1, 3), (0, 4), (3, 2), (2, 3), (1, 4), (3, 3), (2, 4), (3, 4),
 )
+TURN_AT = 3
+PAIRED = {3: ((0, 4), (5, 3)), 4: ((4, 1),)}
 EARLY_LOW = {0: 0}
 MID_LOW = (1, 2, 3)
 LATE_LOW = ()
@@ -70,9 +72,9 @@
 
 
 def kernel(
-    a_ref, g_ref, w_ref, m_ref, new_w_ref, new_m_ref,
+    a_ref, g_ref, out_ref,
     a_vmem, a_t, gathered, high_own, low_own, high_in, low_in, full,
-    gram_own, gram_rep, gram_tp, weights, w_vmem, m_vmem,
+    gram_own, gram_rep, gram_tp, weights,
     load_sem, own_sem, ring_send, ring_recv, pair_send, pair_recv, high_send, high_recv,
     low_send, low_recv, gram_send, gram_recv, greet_sem,
 ):
@@ -101,15 +103,10 @@
     def wait_bytes(ref, sem):
         pltpu.make_async_copy(ref, ref, sem).wait()
 
-    loads = [
-        pltpu.make_async_copy(a_ref, a_vmem, load_sem.at[0]),
-        pltpu.make_async_copy(w_ref, w_vmem, load_sem.at[1]),
-        pltpu.make_async_copy(m_ref, m_vmem, load_sem.at[2]),
-    ]
-    own_rows = pl.ds(pl.multiple_of(tp * BLOCK, BLOCK), BLOCK)
+    load = pltpu.make_async_copy(a_ref, a_vmem, load_sem)
     own_copies = [
         pltpu.make_async_copy(
-            g_ref.at[:, pl.ds(k * WIDTH, WIDTH)], gathered.at[k, own_rows], own_sem.at[k]
+            g_ref.at[:, pl.ds(k * WIDTH, WIDTH)], gathered.at[k, 0, 0], own_sem.at[k]
         )
         for k in range(CHUNKS)
     ]
@@ -126,46 +123,39 @@
                 greet_sem.at[turn], inc=1, device_id=(in_y[d] + x, tp), device_id_type=MESH
             )
 
-    for copy in loads + own_copies:
+    for copy in [load] + own_copies:
         copy.start()
-    loads[0].wait()
-    for i in range(TOKENS // FEATURES):
-        span = pl.ds(i * FEATURES, FEATURES)
-        a_t[:, span] = a_vmem[span, :].T
     pl.semaphore_wait(barrier, 3 + NX - 1 + 2)
     greet(0)
 
-    def rows_from(distance, start=0, size=BLOCK):
-        source = lax.rem(z + NZ + distance, NZ) * 2 + core
-        return pl.ds(pl.multiple_of(source * BLOCK + start, size), size)
-
     def ring_step(k, stage):
-        for way, to, sign in ((0, ahead, -1), (1, behind, 1)):
+        middle = NZ // 2
+        for way, to in ((0, ahead), (1, behind)):
+            half = pl.ds(way * HALF, HALF)
+            held, next_held = (stage, stage + 1) if way else (-stage % NZ, (-stage - 1) % NZ)
             if stage == 0:
-                rows = own_rows
                 src = g_ref.at[:, pl.ds(k * WIDTH, WIDTH)]
             else:
-                if stage < NZ // 2:
-                    rows = rows_from(sign * stage)
-                else:
-                    rows = rows_from(sign * stage, way * HALF, HALF)
-                src = gathered.at[k, rows]
+                src = gathered.at[k, 0, held]
+                came = gathered.at[k, 0, held, half] if stage == middle else src
                 remote(
-                    src, src, ring_send.at[k], ring_recv.at[k, way, stage - 1], rep, to
+                    came, came, ring_send.at[k], ring_recv.at[k, way, stage - 1], rep, to
                 ).wait_recv()
-            if stage < NZ // 2:
-                sent_rows, sent = rows, src
-                if stage == NZ // 2 - 1:
-                    sent_rows = rows_from(sign * stage, way * HALF, HALF)
-                    sent = gathered.at[k, sent_rows]
+            if stage < middle:
+                dst = gathered.at[k, 0, next_held]
+                if stage == middle - 1:
+                    src, dst = gathered.at[k, 0, held, half], gathered.at[k, 0, next_held, half]
                 remote(
-                    sent, gathered.at[k, sent_rows], ring_send.at[k],
-                    ring_recv.at[k, way, stage], rep, to,
+                    src, dst, ring_send.at[k], ring_recv.at[k, way, stage], rep, to
                 ).start()
-            if stage > 0 or way == 0:
-                remote(
-                    src, gathered.at[k, rows], pair_send.at[k], pair_recv.at[k], rep, sibling
-                ).start()
+        for first, count in PAIRED.get(stage, ()):
+            if first == 0:
+                own_copies[k].wait()
+            slots = pl.ds(first, count)
+            remote(
+                gathered.at[k, 0, slots], gathered.at[k, 1, slots],
+                pair_send.at[k], pair_recv.at[k], rep, sibling,
+            ).start()
 
     def send_rows(own, into, send_sem, recv_sem, k):
         def to(peer):
@@ -191,9 +181,10 @@
         into[k, rep] = own[k, rep]
 
     def send_high(k):
-        own_copies[k].wait()
-        wait_bytes(gathered.at[k, pl.ds(0, TOKENS // 2)], pair_recv.at[k])
-        product = jnp.dot(a_t[...], gathered[k], preferred_element_type=jnp.float32)
+        wait_bytes(gathered.at[k, 1], pair_recv.at[k])
+        product = jnp.dot(
+            a_t[...], gathered[k].reshape(TOKENS, WIDTH), preferred_element_type=jnp.float32
+        )
         product = jnp.concatenate(
             [
                 product[:, p * LANES:(p + 1) * LANES].reshape(N_REP, ROWS, LANES)
@@ -223,6 +214,12 @@
         return total
 
     for i, (k, stage) in enumerate(ORDER):
+        if i == TURN_AT:
+            load.wait()
+            for j in range(N_TP):
+                source = in_z[j % NZ] + (core if j < NZ else 1 - core)
+                rows = pl.ds(pl.multiple_of(source * BLOCK, BLOCK), BLOCK)
+                a_t[:, pl.ds(j * BLOCK, BLOCK)] = a_vmem[rows, :].T
         if i in GREET:
             turn = GREET[i]
             pl.semaphore_wait(greet_sem.at[turn], 2)
@@ -265,11 +262,9 @@
     for k in range(CHUNKS):
         wait_bytes(low_in.at[k, pl.ds(0, N_REP - 1)], low_recv.at[k])
         full[k] += low_in[k].astype(jnp.float32)
-    loads[1].wait()
-    loads[2].wait()
     for k in range(CHUNKS):
-        wait_bytes(gathered.at[k, pl.ds(0, 7 * BLOCK)], ring_send.at[k])
-        wait_bytes(gathered.at[k, pl.ds(0, 8 * BLOCK)], pair_send.at[k])
+        wait_bytes(gathered.at[k, 0, pl.ds(0, NZ - 1)], ring_send.at[k])
+        wait_bytes(gathered.at[k, 0], pair_send.at[k])
         wait_bytes(high_own.at[k, pl.ds(0, N_REP - 1)], high_send.at[k])
         wait_bytes(low_own.at[k, pl.ds(0, N_REP - 1)], low_send.at[k])
     wait_bytes(gram_tp.at[pl.ds(0, N_TP - 1)], gram_send.at[0])
@@ -282,27 +277,21 @@
             combined += weights[pl.ds(r, 1), :] * full[k, r]
         for p in range(PARTS):
             span = pl.ds(k * WIDTH + p * LANES, LANES)
-            new_m = MOMENTUM_DECAY * m_vmem[:, span] + combined[p * ROWS:(p + 1) * ROWS]
-            new_m_ref[:, span] = new_m
-            new_w = w_vmem[:, span].astype(jnp.float32) - LEARNING_RATE * new_m
-            new_w_ref[:, span] = new_w.astype(jnp.bfloat16)
+            out_ref[:, span] = combined[p * ROWS:(p + 1) * ROWS]
     wait_bytes(gram_rep.at[pl.ds(0, N_REP - 1)], gram_send.at[1])
 
 
 def body(activations, out_grad, weight, momentum):
     dma = pltpu.SemaphoreType.DMA
-    return pl.pallas_call(
+    combined = pl.pallas_call(
         kernel,
-        out_shape=(
-            jax.ShapeDtypeStruct(weight.shape, jnp.bfloat16),
-            jax.ShapeDtypeStruct(momentum.shape, jnp.float32),
-        ),
-        in_specs=[pl.BlockSpec(memory_space=pltpu.HBM)] * 4,
-        out_specs=(pl.BlockSpec(memory_space=pltpu.VMEM),) * 2,
+        out_shape=jax.ShapeDtypeStruct(momentum.shape, jnp.float32),
+        in_specs=[pl.BlockSpec(memory_space=pltpu.HBM)] * 2,
+        out_specs=pl.BlockSpec(memory_space=pltpu.VMEM),
         scratch_shapes=[
             pltpu.VMEM((TOKENS, FEATURES), jnp.bfloat16),
             pltpu.VMEM((FEATURES, TOKENS), jnp.bfloat16),
-            pltpu.VMEM((CHUNKS, TOKENS, WIDTH), jnp.bfloat16),
+            pltpu.VMEM((CHUNKS, 2, NZ, BLOCK, WIDTH), jnp.bfloat16),
             pltpu.VMEM((CHUNKS, N_REP, PACKED, LANES), jnp.bfloat16),
             pltpu.VMEM((CHUNKS, N_REP, PACKED, LANES), jnp.bfloat16),
             pltpu.VMEM((CHUNKS, N_REP, PACKED, LANES), jnp.bfloat16),
@@ -312,9 +301,7 @@
             pltpu.VMEM((N_REP, ROWS, LANES), jnp.float32),
             pltpu.VMEM((N_TP, ROWS, LANES), jnp.float32),
             pltpu.VMEM((N_REP, LANES), jnp.float32),
-            pltpu.VMEM((ROWS, COLUMNS), jnp.bfloat16),
-            pltpu.VMEM((ROWS, COLUMNS), jnp.float32),
-            dma((3,)),
+            dma,
             dma((CHUNKS,)),
             dma((CHUNKS,)),
             dma((CHUNKS, 2, NZ // 2)),
@@ -329,9 +316,12 @@
             pltpu.SemaphoreType.REGULAR((NY // 2,)),
         ],
         compiler_params=pltpu.CompilerParams(
-            collective_id=0, has_side_effects=True, vmem_limit_bytes=62 * 1024 * 1024
+            collective_id=0, has_side_effects=True, vmem_limit_bytes=56488960
         ),
-    )(activations, out_grad, weight, momentum)
+    )(activations, out_grad)
+    new_momentum = MOMENTUM_DECAY * momentum + combined
+    new_weight = weight.astype(jnp.float32) - LEARNING_RATE * new_momentum
+    return new_weight.astype(jnp.bfloat16), new_momentum
 
 
 def solution(mesh):

time: 65.6 us -> 63.6 us (0.970)
  local copies, waits for them, and re-layouts: 1.95 us -> 0.01 us
  Pallas kernels: 62.8 us -> 62.1 us
    unnamed x4, local copies, waits for them, and re-layouts: 1.95 us -> 0.01 us
where the time goes in v4:
time: 63.6 us; the launch traced here: 63.4 us
  Pallas kernels  62.1 us (98%)
  between operations  0.67 us (1%)
    pallas_call x1, Pallas kernels, body(): pl.pallas_call(kernel, out_shape=jax.ShapeDtypeStruct(momentum.shape, jnp...  62.1 us

profile of v4, /device:TPU:1, one launch (start us, length us, event | category | flops | bytes accessed | tf_op | source)
XLA Modules:
  0.0 63.4 jit_solution(10937614958445058431)
XLA Ops:
  0.6 0.0 copy-start
  0.6 0.0 copy-start.1
  0.7 62.1 %shard_map.59 = f32[8,1024]{1,0:T(8,128)S(1)} custom-call(bf16[2048,256]{1,0:T(8,128)(2,1)} %a_ref.1, bf16[128,1024]{1,0:T(8,128)(2,1)} %g_ref.1), custom_call_target="tpu_custom_call" | custom-call | tf_op jit(solution)/shard_map/pallas_call | solution.py:286
  62.8 0.0 copy-done
  62.8 0.0 copy-done.1
  62.8 0.6 subtract_convert_fusion
Async XLA Ops:
  0.6 62.2 %copy-start = (f32[8,1024]{1,0:T(8,128)S(1)}, f32[8,1024]{1,0:T(8,128)}, u32[]{:S(2)}) copy-start(f32[8,1024]{1,0:T(8,128)} %param.7) | copy-start | bytes 98308
  0.6 62.2 %copy-start.1 = (bf16[8,1024]{1,0:T(8,128)(2,1)S(1)}, bf16[8,1024]{1,0:T(8,128)(2,1)}, u32[]{:S(2)}) copy-start(bf16[8,1024]{1,0:T(8,128)(2,1)} %param.6) | copy-start | bytes 49156

commit v5 on v4

--- a/solution.py
+++ b/solution.py
@@ -34,7 +34,7 @@
     (3, 1), (2, 2), (1, 3), (0, 4), (3, 2), (2, 3), (1, 4), (3, 3), (2, 4), (3, 4),
 )
 TURN_AT = 3
-PAIRED = {3: ((0, 4), (5, 3)), 4: ((4, 1),)}
+PAIRED = {4: ((0, 8),)}
 EARLY_LOW = {0: 0}
 MID_LOW = (1, 2, 3)
 LATE_LOW = ()
@@ -53,12 +53,16 @@
     weights = jnp.ones((N_REP, LANES), jnp.float32)
     for level in range(N_REP.bit_length() - 1):
         apart = 1 << level
-        norm = jnp.sum(jnp.where(diagonal, block, 0.0), axis=0, keepdims=True)
-        inner = jnp.sum(jnp.where(row == (column ^ apart), block, 0.0), axis=0, keepdims=True)
-        across = jnp.broadcast_to(1.0 - inner / (2.0 * norm), (N_REP, LANES))
-        down = jnp.sum(jnp.where(row == lane, across, 0.0), axis=1, keepdims=True)
-        down = jnp.broadcast_to(down, (N_REP, LANES))
+        own, other = jnp.where(diagonal, block, 0.0), jnp.where(row == (column ^ apart), block, 0.0)
+        across = 1.0 - jnp.sum(other, axis=0, keepdims=True) / (
+            2.0 * jnp.sum(own, axis=0, keepdims=True)
+        )
+        down = 1.0 - jnp.sum(other, axis=1, keepdims=True) / (
+            2.0 * jnp.sum(own, axis=1, keepdims=True)
+        )
         weights = weights * down
+        if apart == N_REP // 2:
+            break
         block = block * across * down
         upper = (column & apart) != 0
         block = block + jnp.where(

time: 63.6 us -> 63.4 us (level)
  no operation moved by 1% of the time
where the time goes in v5:
time: 63.4 us; the launch traced here: 63.2 us
  Pallas kernels  61.9 us (98%)
  between operations  0.67 us (1%)
    pallas_call x1, Pallas kernels, body(): pl.pallas_call(kernel, out_shape=jax.ShapeDtypeStruct(momentum.shape, jnp...  61.9 us

profile of v5, /device:TPU:1, one launch (start us, length us, event | category | flops | bytes accessed | tf_op | source)
XLA Modules:
  0.0 63.2 jit_solution(12222545570057815598)
XLA Ops:
  0.6 0.0 copy-start
  0.6 0.0 copy-start.1
  0.7 61.9 %shard_map.59 = f32[8,1024]{1,0:T(8,128)S(1)} custom-call(bf16[2048,256]{1,0:T(8,128)(2,1)} %a_ref.1, bf16[128,1024]{1,0:T(8,128)(2,1)} %g_ref.1), custom_call_target="tpu_custom_call" | custom-call | tf_op jit(solution)/shard_map/pallas_call | solution.py:290
  62.6 0.0 copy-done
  62.6 0.0 copy-done.1
  62.6 0.6 subtract_convert_fusion
Async XLA Ops:
  0.6 62.0 %copy-start = (f32[8,1024]{1,0:T(8,128)S(1)}, f32[8,1024]{1,0:T(8,128)}, u32[]{:S(2)}) copy-start(f32[8,1024]{1,0:T(8,128)} %param.7) | copy-start | bytes 98308
  0.6 62.0 %copy-start.1 = (bf16[8,1024]{1,0:T(8,128)(2,1)S(1)}, bf16[8,1024]{1,0:T(8,128)(2,1)}, u32[]{:S(2)}) copy-start(bf16[8,1024]{1,0:T(8,128)(2,1)} %param.6) | copy-start | bytes 49156
